TPU v7x, 32 devices: a whole 2x2x4 slice. The times are simulated.
32 devices in a mesh: seq: 4 (over z), fsdp: 8 (over y, x, core).
Axes of the slice: x: 2, y: 2, z: 4, core: 2. Of those that a mesh axis runs over, the one named last changes fastest.
Arguments:
- tokens: float32 [2, 8, 1024, 1024], P(None, 'fsdp', 'seq'), may hold values from -6 to 6
- cotangent: float32 [2, 8, 1024, 1024], P(None, 'fsdp', 'seq'), may hold values from -6 to 6
- doc_starts: int32 [2, 8, 8], P(None, 'fsdp'), may hold values from 0 to 1023, as said below
- qkv_weight: bfloat16 [1024, 3072], P('fsdp'), may hold values from -0.1875 to 0.1875
- out_weight: bfloat16 [1024, 1024], P('fsdp'), may hold values from -3.5 to 3.5
- in_weight: bfloat16 [1024, 5248], P('fsdp'), may hold values from -0.1875 to 0.1875
- down_weight: bfloat16 [2624, 1024], P('fsdp'), may hold values from -0.125 to 0.125
- attn_gain: bfloat16 [1024], P('fsdp'), may hold values from 0.5 to 1.5
- ffn_gain: bfloat16 [1024], P('fsdp'), may hold values from 0.5 to 1.5
Outputs:
- output: float32 [2, 8, 1024, 1024], P(None, 'fsdp', 'seq')
- tokens_grad: float32 [2, 8, 1024, 1024], P(None, 'fsdp', 'seq')
- qkv_grad: float32 [1024, 3072], P('fsdp')
- out_grad: float32 [1024, 1024], P('fsdp')
- in_grad: float32 [1024, 5248], P('fsdp')
- down_grad: float32 [2624, 1024], P('fsdp')
- attngain_grad: float32 [1024], P('fsdp')
- ffngain_grad: float32 [1024], P('fsdp')
Inputs may be any that keep to these rules, and one draw needn't show every extreme that they name: `doc_starts`: in every stream the starts rise strictly from 0 and stay below 1024; one document of every stream begins within the first 256 positions and ends within the last 256 positions.
All inputs are finite; a program needn't handle non-finite values.
Results may differ from a plain program's by a relative error of at most 0.02.
Values may be sent and summed in bfloat16 or wider, within the bound.
A program may use at most 192 MiB of HBM per device.

v0:
```python
from functools import partial

import jax
import jax.numpy as jnp
from jax import lax
from jax.sharding import PartitionSpec as P

HEADS = 16
HEAD_DIM = 64


EPSILON = 1e-05
ROPE_THETA = 160000.0
MASKED_SCORE = -1e30


def as_sent(x):

    def short(part):
        return part.astype(jnp.bfloat16) if part.dtype == jnp.float32 else part

    return jax.tree.map(short, x)


def layer_norm(values, norm_gain):
    average = jnp.mean(values, axis=-1, keepdims=True)
    centred = values - average
    spread = jnp.mean(centred * centred, axis=-1, keepdims=True)
    return centred * lax.rsqrt(spread + EPSILON) * norm_gain


def gated_gelu(joined):
    half_width = joined.shape[-1] // 2
    return jax.nn.gelu(joined[:, :half_width], approximate=False) * joined[:, half_width:]


def rotate(values, cosine_table, sine_table):
    half_width = values.shape[-1] // 2
    turned = jnp.concatenate([-values[..., half_width:], values[..., :half_width]], axis=-1)
    return values * cosine_table + turned * sine_table


def rope_tables(starts, places, head_width):
    preceding = starts[None, :] <= places[:, None]
    doc_begin = jnp.max(jnp.where(preceding, starts[None, :], 0), axis=-1)
    offsets = (places - doc_begin).astype(jnp.float32)
    inverse = ROPE_THETA ** (-jnp.arange(0, head_width, 2, dtype=jnp.float32) / head_width)
    angles = offsets[:, None] * inverse[None, :]
    angles = jnp.concatenate([angles, angles], axis=-1)
    return (jnp.cos(angles), jnp.sin(angles))


def segment_ids(starts, places):
    return jnp.sum((starts[None, :] <= places[:, None]).astype(jnp.int32), axis=-1) - 1


def turn_pair(pair, cosine_table, sine_table):
    shaped = pair.reshape(pair.shape[0], 2, HEADS, HEAD_DIM)
    turned = rotate(shaped, cosine_table[:, None, None, :], sine_table[:, None, None, :])
    return turned.reshape(pair.shape[0], 2 * HEADS * HEAD_DIM)


def attend_forward(queries, keys_in, values_in, segments, head_count):
    length = queries.shape[0]
    head_width = queries.shape[1] // head_count
    block_rows = min(512, length)
    blocks = length // block_rows
    keyset = keys_in.reshape(length, head_count, head_width)
    valueset = values_in.reshape(length, head_count, head_width)
    factor = head_width ** (-0.5)

    def one_block(pieces):
        query_rows, block_segs = pieces
        scores = (
            jnp.einsum("qhd,khd->hqk", query_rows, keyset, preferred_element_type=jnp.float32)
            * factor
        )
        scores = jnp.where((block_segs[:, None] == segments[None, :])[None], scores, MASKED_SCORE)
        row_max = jnp.max(scores, axis=-1, keepdims=True)
        totals = jnp.sum(jnp.exp(scores - row_max), axis=-1, keepdims=True)
        logsums = row_max + jnp.log(totals)
        weights = jnp.exp(scores - logsums).astype(jnp.bfloat16)
        mixture = jnp.einsum("hqk,khd->qhd", weights, valueset, preferred_element_type=jnp.float32)
        return (mixture, logsums)

    mixture, logsums = lax.map(
        one_block,
        (
            queries.reshape(blocks, block_rows, head_count, head_width),
            segments.reshape(blocks, block_rows),
        ),
    )
    return (mixture.reshape(length, head_count * head_width), logsums)


def attend_backward(queries, keys_in, values_in, grads_in, segments, logsums, head_count):
    length = queries.shape[0]
    head_width = queries.shape[1] // head_count
    block_rows = min(512, length)
    blocks = length // block_rows
    keyset = keys_in.reshape(length, head_count, head_width)
    valueset = values_in.reshape(length, head_count, head_width)
    factor = head_width ** (-0.5)

    def one_block(carry, pieces):
        key_grad, value_grad = carry
        query_rows, block_segs, grad_rows, block_lse = pieces
        scores = (
            jnp.einsum("qhd,khd->hqk", query_rows, keyset, preferred_element_type=jnp.float32)
            * factor
        )
        scores = jnp.where((block_segs[:, None] == segments[None, :])[None], scores, MASKED_SCORE)
        weights = jnp.exp(scores - block_lse)
        value_grad = value_grad + jnp.einsum(
            "hqk,qhd->khd",
            weights.astype(jnp.bfloat16),
            grad_rows,
            preferred_element_type=jnp.float32,
        )
        grad_weights = jnp.einsum(
            "qhd,khd->hqk", grad_rows, valueset, preferred_element_type=jnp.float32
        )
        centre = jnp.sum(weights * grad_weights, axis=-1, keepdims=True)
        grad_scores = (weights * (grad_weights - centre)).astype(jnp.bfloat16)
        query_grad = (
            jnp.einsum("hqk,khd->qhd", grad_scores, keyset, preferred_element_type=jnp.float32)
            * factor
        )
        key_grad = (
            key_grad
            + jnp.einsum(
                "hqk,qhd->khd", grad_scores, query_rows, preferred_element_type=jnp.float32
            )
            * factor
        )
        return ((key_grad, value_grad), query_grad)

    empty = jnp.zeros((length, head_count, head_width), jnp.float32)
    pieces = (
        queries.reshape(blocks, block_rows, head_count, head_width),
        segments.reshape(blocks, block_rows),
        grads_in.reshape(blocks, block_rows, head_count, head_width),
        logsums,
    )
    (key_grad, value_grad), query_grad = lax.scan(one_block, (empty, empty), pieces)
    flat_shape = (length, head_count * head_width)
    return (
        query_grad.reshape(flat_shape).astype(jnp.bfloat16),
        key_grad.reshape(flat_shape).astype(jnp.bfloat16),
        value_grad.reshape(flat_shape).astype(jnp.bfloat16),
    )


def shards(
    tokens,
    cotangent,
    doc_starts,
    qkv_weight,
    out_weight,
    in_weight,
    down_weight,
    attn_gain,
    ffn_gain,
):
    micro_count = tokens.shape[0]
    token_rows = tokens.shape[2]
    model_width = tokens.shape[3]
    seq_count = lax.axis_size("seq")
    head_count = HEADS // seq_count
    places = lax.axis_index("seq") * token_rows + jnp.arange(token_rows, dtype=jnp.int32)
    everywhere = jnp.arange(token_rows * seq_count, dtype=jnp.int32)
    outputs = []
    input_grads = []
    full_terms = None
    shard_terms = None
    for micro_step in range(micro_count):
        rows_in = tokens[micro_step, 0]
        starts = doc_starts[micro_step, 0]
        cosine_table, sine_table = rope_tables(starts, places, HEAD_DIM)
        segments = segment_ids(starts, everywhere)
        attn_set = (
            lax.all_gather(qkv_weight, "fsdp", axis=0, tiled=True),
            lax.all_gather(out_weight, "fsdp", axis=0, tiled=True),
            lax.all_gather(attn_gain, "fsdp", axis=0, tiled=True),
        )
        qkv_full, out_full, gain_one = attn_set
        normed, norm_back = jax.vjp(layer_norm, rows_in, gain_one.astype(jnp.float32))
        normed_low = normed.astype(jnp.bfloat16)
        qkv_rows = jnp.dot(normed_low, qkv_full, preferred_element_type=jnp.float32)
        turned, turn_back = jax.vjp(
            partial(turn_pair, cosine_table=cosine_table, sine_table=sine_table),
            qkv_rows[:, : 2 * model_width],
        )
        queries = turned[:, :model_width].astype(jnp.bfloat16)
        keyset = turned[:, model_width:].astype(jnp.bfloat16)
        valueset = qkv_rows[:, 2 * model_width :].astype(jnp.bfloat16)
        query_heads, key_heads, value_heads = (
            lax.all_to_all(queries, "seq", split_axis=1, concat_axis=0, tiled=True),
            lax.all_to_all(keyset, "seq", split_axis=1, concat_axis=0, tiled=True),
            lax.all_to_all(valueset, "seq", split_axis=1, concat_axis=0, tiled=True),
        )
        mixture, logsums = attend_forward(query_heads, key_heads, value_heads, segments, head_count)
        mixture_rows = lax.all_to_all(
            mixture.astype(jnp.bfloat16), "seq", split_axis=0, concat_axis=1, tiled=True
        )
        middle = rows_in + jnp.dot(mixture_rows, out_full, preferred_element_type=jnp.float32)
        ffn_set = (
            lax.all_gather(in_weight, "fsdp", axis=0, tiled=True),
            lax.all_gather(down_weight, "fsdp", axis=0, tiled=True),
            lax.all_gather(ffn_gain, "fsdp", axis=0, tiled=True),
        )
        in_full, down_full, gain_two = ffn_set
        normed_two, norm_back_two = jax.vjp(layer_norm, middle, gain_two.astype(jnp.float32))
        normed_two_low = normed_two.astype(jnp.bfloat16)
        joined = jnp.dot(normed_two_low, in_full, preferred_element_type=jnp.float32)
        active, gelu_back = jax.vjp(gated_gelu, joined)
        active_low = active.astype(jnp.bfloat16)
        outputs.append(middle + jnp.dot(active_low, down_full, preferred_element_type=jnp.float32))
        grad_out = cotangent[micro_step, 0]
        grad_low = grad_out.astype(jnp.bfloat16)
        ffn_set = (
            lax.all_gather(in_weight, "fsdp", axis=0, tiled=True),
            lax.all_gather(down_weight, "fsdp", axis=0, tiled=True),
            lax.all_gather(ffn_gain, "fsdp", axis=0, tiled=True),
        )
        in_full, down_full, gain_two = ffn_set
        down_term = jnp.dot(active_low.T, grad_low, preferred_element_type=jnp.float32)
        grad_active = jnp.dot(grad_low, down_full.T, preferred_element_type=jnp.float32)
        grad_joined = gelu_back(grad_active)[0].astype(jnp.bfloat16)
        in_term = jnp.dot(normed_two_low.T, grad_joined, preferred_element_type=jnp.float32)
        grad_normed_two = jnp.dot(grad_joined, in_full.T, preferred_element_type=jnp.float32)
        grad_middle_norm, gain_two_term = norm_back_two(grad_normed_two)
        grad_middle = grad_out + grad_middle_norm
        grad_mid_low = grad_middle.astype(jnp.bfloat16)
        attn_set = (
            lax.all_gather(qkv_weight, "fsdp", axis=0, tiled=True),
            lax.all_gather(out_weight, "fsdp", axis=0, tiled=True),
            lax.all_gather(attn_gain, "fsdp", axis=0, tiled=True),
        )
        qkv_full, out_full, gain_one = attn_set
        out_term = jnp.dot(mixture_rows.T, grad_mid_low, preferred_element_type=jnp.float32)
        grad_mixture = jnp.dot(grad_mid_low, out_full.T, preferred_element_type=jnp.float32).astype(
            jnp.bfloat16
        )
        grad_heads = lax.all_to_all(grad_mixture, "seq", split_axis=1, concat_axis=0, tiled=True)
        query_grad, key_grad, value_grad = attend_backward(
            query_heads, key_heads, value_heads, grad_heads, segments, logsums, head_count
        )
        query_back, key_back, value_back = (
            lax.all_to_all(query_grad, "seq", split_axis=0, concat_axis=1, tiled=True),
            lax.all_to_all(key_grad, "seq", split_axis=0, concat_axis=1, tiled=True),
            lax.all_to_all(value_grad, "seq", split_axis=0, concat_axis=1, tiled=True),
        )
        grad_pair = turn_back(jnp.concatenate([query_back, key_back], axis=1).astype(jnp.float32))[
            0
        ]
        grad_qkv = jnp.concatenate([grad_pair, value_back.astype(jnp.float32)], axis=1).astype(
            jnp.bfloat16
        )
        qkv_term = jnp.dot(normed_low.T, grad_qkv, preferred_element_type=jnp.float32)
        grad_normed = jnp.dot(grad_qkv, qkv_full.T, preferred_element_type=jnp.float32)
        grad_rows_norm, gain_one_term = norm_back(grad_normed)
        input_grads.append(grad_middle + grad_rows_norm)
        terms = (qkv_term, out_term, in_term, down_term, gain_one_term, gain_two_term)
        full_terms = terms if full_terms is None else jax.tree.map(jnp.add, full_terms, terms)
    shard_terms = jax.tree.map(
        lambda part: part.astype(jnp.float32),
        lax.psum_scatter(as_sent(full_terms), "fsdp", scatter_dimension=0, tiled=True),
    )
    totals = jax.tree.map(
        lambda part: part.astype(jnp.float32), lax.psum(as_sent(shard_terms), "seq")
    )
    return (
        jnp.stack(outputs)[:, None],
        jnp.stack(input_grads)[:, None],
        totals[0],
        totals[1],
        totals[2],
        totals[3],
        totals[4],
        totals[5],
    )


def solution(mesh):
    return jax.shard_map(
        shards,
        mesh=mesh,
        in_specs=(
            P(None, "fsdp", "seq", None),
            P(None, "fsdp", "seq", None),
            P(None, "fsdp", None),
            P("fsdp", None),
            P("fsdp", None),
            P("fsdp", None),
            P("fsdp", None),
            P("fsdp"),
            P("fsdp"),
        ),
        out_specs=(
            P(None, "fsdp", "seq", None),
            P(None, "fsdp", "seq", None),
            P("fsdp", None),
            P("fsdp", None),
            P("fsdp", None),
            P("fsdp", None),
            P("fsdp"),
            P("fsdp"),
        ),
        check_vma=False,
    )
```

profile of v0, /device:TPU:0, one launch (start us, length us, event | category | flops | bytes accessed | tf_op | source)
XLA Modules:
  0.0 834.2 jit_solution(12347422703129561592)
XLA Ops:
  9.4 10.3 %all-gather = bf16[8,1,128]{2,1,0:T(2,128)(2,1)S(1)} all-gather(bf16[1,1,128]{2,1,0:T(2,128)(2,1)} %bitcast.408), channel_id=1, replica_groups=mesh['seq'=4,'fsdp'=8] {'fsdp'}, dimensions={0}, use_global_device_ids=true | all-gather | bytes 2304 | tf_op jit(solution)/shard_map/all_gather | solution.py:184
  26.4 31.7 %all-gather.7.cloned.1.call-done = bf16[1024,3072]{1,0:T(8,128)(2,1)} async-done(((bf16[128,3072]{1,0:T(8,128)(2,1)}), bf16[1024,3072]{1,0:T(8,128)(2,1)}) %all-gather.7.cloned.1.call-update) | async-done | bytes 6291472 | tf_op jit(solution)/shard_map/all_gather | solution.py:182
  90.2 8.9 %all-to-all-done.4 = bf16[256,4,256]{0,2,1:T(8,128)(2,1)S(1)} async-done(((bf16[256,4,256]{0,2,1:T(8,128)(2,1)}), bf16[256,4,256]{0,2,1:T(8,128)(2,1)S(1)}, u32[]{:S(2)}, u32[]{:S(2)}) %all-to-all-start.4) | async-done | bytes 524320 | tf_op jit(solution)/shard_map/all_to_all | solution.py:198
  127.2 9.9 %all-to-all-done.6 = bf16[256,4,256]{2,0,1:T(8,128)(2,1)} async-done(((bf16[256,4,256]{2,0,1:T(8,128)(2,1)}), bf16[256,4,256]{2,0,1:T(8,128)(2,1)}, u32[]{:S(2)}, u32[]{:S(2)}) %all-to-all-start.6) | async-done | bytes 524320 | tf_op jit(solution)/shard_map/all_to_all | solution.py:200
  141.4 13.2 %all-to-all-done = bf16[256,4,256]{0,2,1:T(8,128)(2,1)S(1)} async-done(((bf16[256,4,256]{0,2,1:T(8,128)(2,1)}), bf16[256,4,256]{0,2,1:T(8,128)(2,1)S(1)}, u32[]{:S(2)}, u32[]{:S(2)}) %all-to-all-start) | async-done | bytes 524320 | tf_op jit(solution)/shard_map/all_to_all | solution.py:198
  176.3 15.1 %while.55 = (s32[]{:T(128)}, bf16[2,512,4,64]{1,3,2,0:T(8,128)(2,1)}, f32[2,4,512,1]{2,1,3,0:T(4,128)S(1)}, s32[2,512]{1,0:T(2,128)S(1)}, s32[1024]{0:T(1024)S(1...) while((s32[]{:T(128)}, ...), condition=%wide.region_17.18_spmd, body=%wide.region_14.17_spmd.sunk | while | flops 560461824 | bytes 33368236 | solution.py:86
  211.4 15.1 %while.54 = (s32[]{:T(128)}, bf16[2,512,4,64]{1,3,2,0:T(8,128)(2,1)}, f32[2,4,512,1]{2,1,3,0:T(4,128)S(1)}, s32[2,512]{1,0:T(2,128)S(1)}, s32[1024]{0:T(1024)S(1...) while((s32[]{:T(128)}, ...), condition=%wide.region_7.8_spmd, body=%wide.region_4.7_spmd.sunk | while | flops 560461824 | bytes 33368236 | solution.py:86
  253.7 9.8 %fusion.137 = f32[256,5248]{1,0:T(8,128)} fusion(bf16[1024,5248]{1,0:T(8,128)(2,1)} %all-gather.11.cloned.1.call-done, f32[256,1024]{1,0:T(8,128)} %copy-done.15, f32[256]{0:T(256)S(1)} %fusion.127, f32[256]{0:T(256)S(1)} %broadcast_multiply_fusion.2, f32[1024]{0:T(1024)S(1)} %bitcast.392), kind=kOutput, calls=%fused_computation.283 | convolution fusion | flops 2752512000 | bytes 17176576 | tf_op jit(solution)/shard_map/dot_general | solution.py:215
  263.6 13.2 %fusion.107 = (f32[256,2624]{1,0:T(8,128)}, f32[256,2624]{1,0:T(8,128)}, f32[256,2624]{1,0:T(8,128)}) fusion(f32[256,5248]{1,0:T(8,128)} %fusion.137, bf16[2624,1024]{1,0:T(8,128)(2,1)} %all-gather.13.cloned.1.call-done, f32[2,1,256,1024]{3,2,1,0:T(8,128)} %param.18), kind=kOutput, calls=%fused_computation.213 | convolution fusion | flops 1419395072 | bytes 16711680 | tf_op jit(solution)/shard_map/dot_general | solution.py:228
  287.3 11.0 %fusion.108 = (f32[256,2624]{1,0:T(8,128)}, f32[256,2624]{1,0:T(8,128)S(1)}, f32[256,2624]{1,0:T(8,128)S(1)}) fusion(f32[256,5248]{1,0:T(8,128)S(1)} %fusion.136, bf16[2624,1024]{1,0:T(8,128)(2,1)} %all-gather.13.cloned.1.call-done, f32[2,1,256,1024]{3,2,1,0:T(8,128)S(1)} %copy-done.31), kind=kOutput, calls=%fused_computation.214 | convolution fusion | flops 1419395072 | bytes 16711680 | tf_op jit(solution)/shard_map/dot_general | solution.py:228
  301.8 9.8 %fusion.111 = f32[256,1024]{1,0:T(8,128)} fusion(bf16[1024,5248]{1,0:T(8,128)(2,1)} %all-gather.11.cloned.1.call-done, f32[256,2624]{1,0:T(8,128)} %get-tuple-element.658, f32[256,2624]{1,0:T(8,128)} %get-tuple-element.646), kind=kOutput, calls=%fused_computation.221 | convolution fusion | flops 2754150400 | bytes 17170432 | tf_op jit(solution)/shard_map/dot_general | solution.py:231
  311.6 11.1 %multiply_reduce_fusion.3 = (f32[1024]{0:T(1024)}, f32[256]{0:T(256)S(1)}, f32[256]{0:T(256)S(1)}, f32[1024]{0:T(1024)}, f32[256,1024]{1,0:T(8,128)}) fusion(f32[256,1024]{1,0:T(8,128)S(1)} %copy-done.19, f32[256]{0:T(256)S(1)} %fusion.125, f32[256]{0:T(256)S(1)} %broadcast_multiply_fusion.4, f32[1024]{0:T(1024)S(1)} %bitcast.394, ...), kind=kOutput, calls=%fused_computation.191 | convolution fusion | flops 2757817856 | bytes 20334592 | tf_op jit(solution)/shard_map/dot_general | solution.py:231
  358.8 39.5 %while.57 = (s32[]{:T(128)}, f32[1024,4,64]{0,2,1:T(8,128)S(1)}, f32[1024,4,64]{0,2,1:T(8,128)}, bf16[2,512,4,64]{1,3,2,0:T(8,128)(2,1)}, bf16[2,512,4,64]{1,3,2...) while((s32[]{:T(128)}, f32[1024,4,64]{0,2,1:T(8,128)S(1)}, ...), condition=%wide.region_31.32_spmd.clone, body=%wide.region_29.31_spmd.clone.sunk | while | flops 1375598592 | bytes 164694384 | solution.py:145
  427.9 40.4 %while.56 = (s32[]{:T(128)}, f32[1024,4,64]{0,2,1:T(8,128)S(1)}, f32[1024,4,64]{0,2,1:T(8,128)}, bf16[2,512,4,64]{1,3,2,0:T(8,128)(2,1)}, bf16[2,512,4,64]{1,3,2...) while((s32[]{:T(128)}, f32[1024,4,64]{0,2,1:T(8,128)S(1)}, ...), condition=%wide.region_24.25_spmd.clone, body=%wide.region_22.24_spmd.clone.sunk | while | flops 1375598592 | bytes 164694384 | solution.py:145
  476.3 11.6 %all-to-all-done.10 = bf16[4,256,256]{1,2,0:T(8,128)(2,1)S(1)} async-done(((bf16[4,256,256]{1,2,0:T(8,128)(2,1)}), bf16[4,256,256]{1,2,0:T(8,128)(2,1)S(1)}, u32[]{:S(2)}, u32[]{:S(2)}) %all-to-all-start.10) | async-done | bytes 524320 | tf_op jit(solution)/shard_map/all_to_all | solution.py:251
  513.9 9.6 %all-to-all-done.11 = bf16[4,256,256]{1,2,0:T(8,128)(2,1)} async-done(((bf16[4,256,256]{1,2,0:T(8,128)(2,1)}), bf16[4,256,256]{1,2,0:T(8,128)(2,1)}, u32[]{:S(2)}, u32[]{:S(2)}) %all-to-all-start.11) | async-done | bytes 524320 | tf_op jit(solution)/shard_map/all_to_all | solution.py:252
  541.7 9.3 %add_convert_fusion.1 = bf16[1024,3072]{1,0:T(8,128)(2,1)} fusion(f32[1024,3072]{1,0:T(8,128)} %fusion.105, bf16[256,1024]{0,1:T(8,128)(2,1)} %bitcast.60, bf16[256,2048]{0,1:T(8,128)(2,1)S(1)} %bitcast.377, f32[2,1,256,1024]{3,2,1,0:T(8,128)S(1)} %copy-done.10, f32[256]{0:T(256)S(1)} %copy-done.97, f32[256]{0:T(256)S(1)} %copy-done.91, f32[1024]{0:T(1024)S(1)} %bitcast.405), kind=kOutput, calls=%fused_computation.103 | convolution fusion | flops 1621098496 | bytes 21501952 | tf_op jit(solution)/shard_map/dot_general | solution.py:260
  551.7 15.2 %fusion.109 = f32[1024,5248]{1,0:T(8,128)} fusion(f32[256,2624]{1,0:T(8,128)} %get-tuple-element.656, f32[256,2624]{1,0:T(8,128)} %get-tuple-element.642, f32[256,1024]{1,0:T(8,128)} %copy-done.18, f32[1024]{0:T(1024)S(1)} %bitcast.396, f32[256]{0:T(256)S(1)} %copy-done.81, f32[256]{0:T(256)S(1)} %copy-done.79), kind=kOutput, calls=%fused_computation.219 | convolution fusion | flops 2755198976 | bytes 27924480 | tf_op jit(solution)/shard_map/dot_general | solution.py:230
  566.9 15.9 %add_convert_fusion = bf16[1024,5248]{1,0:T(8,128)(2,1)} fusion(f32[1024,5248]{1,0:T(8,128)} %fusion.109, f32[256,2624]{1,0:T(8,128)} %get-tuple-element.658, f32[256,2624]{1,0:T(8,128)} %get-tuple-element.646, f32[256,1024]{1,0:T(8,128)S(1)} %copy-done.17, f32[256]{0:T(256)S(1)} %copy-done.85, f32[256]{0:T(256)S(1)} %copy-done.83, f32[1024]{0:T(1024)S(1)} %bitcast.397), kind=kOutput, calls=%fused_computation.102 | convolution fusion | flops 2765946880 | bytes 38672384 | tf_op jit(solution)/shard_map/dot_general | solution.py:230
  595.4 15.6 %reduce-scatter.5.cloned.1.call-done = bf16[128,3072]{1,0:T(8,128)(2,1)} async-done(((bf16[1024,3072]{1,0:T(8,128)(2,1)}), bf16[128,3072]{1,0:T(8,128)(2,1)}) %reduce-scatter.5.cloned.1.call-update) | async-done | bytes 786448 | tf_op jit(solution)/shard_map/reduce_scatter | solution.py:268
  611.0 86.3 %reduce-scatter.9.cloned.1.call-done = bf16[128,5248]{1,0:T(8,128)(2,1)} async-done(((bf16[1024,5248]{1,0:T(8,128)(2,1)}), bf16[128,5248]{1,0:T(8,128)(2,1)}) %reduce-scatter.9.cloned.1.call-update) | async-done | bytes 1343504 | tf_op jit(solution)/shard_map/reduce_scatter | solution.py:268
  708.0 13.5 %all-reduce.10 = (bf16[1024]{0:T(1024)(128)(2,1)S(1)}, bf16[1024]{0:T(1024)(128)(2,1)S(1)}) all-reduce(bf16[1024]{0:T(1024)(128)(2,1)S(1)} %add_convert_fusion.13, bf16[1024]{0:T(1024)(128)(2,1)S(1)} %add_convert_fusion.12), channel_id=6, replica_groups=mesh['seq'=4,'fsdp'=8] {'fsdp'}, use_global_device_ids=true, to_apply=%region_44.45.clone | all-reduce | flops 2048 | bytes 8192
  721.7 12.4 %all-reduce.11 = (bf16[128]{0:T(256)(128)(2,1)S(1)}, bf16[128]{0:T(256)(128)(2,1)S(1)}) all-reduce(bf16[128]{0:T(256)(128)(2,1)S(1)} %dynamic-slice.1, bf16[128]{0:T(256)(128)(2,1)S(1)} %dynamic-slice.3), channel_id=1, replica_groups=mesh['seq'=4,'fsdp'=8] {'seq'}, use_global_device_ids=true, to_apply=%region_45.46 | all-reduce | flops 256 | bytes 1024 | tf_op jit(solution)/shard_map/psum | solution.py:271
  740.0 80.1 %all-reduce.15.cloned.1.call-done = (bf16[128,3072]{1,0:T(8,128)(2,1)}, bf16[128,1024]{1,0:T(8,128)(2,1)}, bf16[128,5248]{1,0:T(8,128)(2,1)}, bf16[328,1024]{1,0:T(8,128)(2,1)}) async-done(((bf16[128,3072]{1,0:T(8,128)(2,1)}, bf16[128,1024]{1,0:T(8,128)(2,1)}, bf16[128,5248]{1,0:T(8,128)(2,1)}, bf16[328,1024]{1,0:T(8,128)(2,1)}), (bf16[128,3072]{1,0:T(8,128)(2,1)}, bf16[128,1024]{1,0:T(8,128)(2,1)}, ...) | async-done | bytes 3063824 | tf_op jit(solution)/shard_map/psum | solution.py:271
  (510 shorter events, 419.2 us)
Async XLA Ops:
  7.2 51.0 %all-gather.7.cloned.1.call-start = ((), (), s32[]{:S(2)}) async-start(), calls=%async_computation.20 | async-start | bytes 7077888 | tf_op jit(solution)/shard_map/all_gather | solution.py:182
  7.9 237.5 %all-gather.9.cloned.1.call-start = ((), (), s32[]{:S(2)}) async-start(), calls=%async_computation.21 | async-start | bytes 2359296 | tf_op jit(solution)/shard_map/all_gather | solution.py:183
  8.7 245.1 %all-gather.11.cloned.1.call-start = ((), (), s32[]{:S(2)}) async-start(), calls=%async_computation.22 | async-start | bytes 12091392 | tf_op jit(solution)/shard_map/all_gather | solution.py:208
  79.5 19.5 %all-to-all-start.4 = ((bf16[256,4,256]{0,2,1:T(8,128)(2,1)}), bf16[256,4,256]{0,2,1:T(8,128)(2,1)S(1)}, u32[]{:S(2)}, u32[]{:S(2)}) async-start(bf16[256,4,256]{0,2,1:T(8,128)(2,1)} %bitcast.31), calls=%async_computation.4 | async-start | bytes 1048576 | tf_op jit(solution)/shard_map/all_to_all | solution.py:198
  99.0 19.4 %all-to-all-start.5 = ((bf16[256,4,256]{2,0,1:T(8,128)(2,1)}), bf16[256,4,256]{2,0,1:T(8,128)(2,1)S(1)}, u32[]{:S(2)}, u32[]{:S(2)}) async-start(bf16[256,4,256]{2,0,1:T(8,128)(2,1)} %bitcast.387), calls=%async_computation.5 | async-start | bytes 1048576 | tf_op jit(solution)/shard_map/all_to_all | solution.py:199
  118.4 18.7 %all-to-all-start.6 = ((bf16[256,4,256]{2,0,1:T(8,128)(2,1)}), bf16[256,4,256]{2,0,1:T(8,128)(2,1)}, u32[]{:S(2)}, u32[]{:S(2)}) async-start(bf16[256,4,256]{2,0,1:T(8,128)(2,1)} %bitcast.386), calls=%async_computation.6 | async-start | bytes 1048576 | tf_op jit(solution)/shard_map/all_to_all | solution.py:200
  137.1 17.5 %all-to-all-start = ((bf16[256,4,256]{0,2,1:T(8,128)(2,1)}), bf16[256,4,256]{0,2,1:T(8,128)(2,1)S(1)}, u32[]{:S(2)}, u32[]{:S(2)}) async-start(bf16[256,4,256]{0,2,1:T(8,128)(2,1)} %bitcast.17), calls=%async_computation | async-start | bytes 1048576 | tf_op jit(solution)/shard_map/all_to_all | solution.py:198
  154.6 17.4 %all-to-all-start.1 = ((bf16[256,4,256]{2,0,1:T(8,128)(2,1)}), bf16[256,4,256]{2,0,1:T(8,128)(2,1)S(1)}, u32[]{:S(2)}, u32[]{:S(2)}) async-start(bf16[256,4,256]{2,0,1:T(8,128)(2,1)} %bitcast.286), calls=%async_computation.1 | async-start | bytes 1048576 | tf_op jit(solution)/shard_map/all_to_all | solution.py:199
  158.1 105.5 %all-gather.13.cloned.1.call-start = ((), (), s32[]{:S(2)}) async-start(), calls=%async_computation.23 | async-start | bytes 6045696 | tf_op jit(solution)/shard_map/all_gather | solution.py:209
  172.0 32.4 %all-to-all-start.2 = ((bf16[256,4,256]{2,0,1:T(8,128)(2,1)}), bf16[256,4,256]{2,0,1:T(8,128)(2,1)S(1)}, u32[]{:S(2)}, u32[]{:S(2)}) async-start(bf16[256,4,256]{2,0,1:T(8,128)(2,1)} %bitcast.285), calls=%async_computation.2 | async-start | bytes 1048576 | tf_op jit(solution)/shard_map/all_to_all | solution.py:200
  204.4 27.1 %all-to-all-start.7 = ((bf16[4,256,256]{1,2,0:T(8,128)(2,1)}), bf16[4,256,256]{1,2,0:T(8,128)(2,1)}, u32[]{:S(2)}, u32[]{:S(2)}) async-start(bf16[4,256,256]{1,2,0:T(8,128)(2,1)} %copy.220), calls=%async_computation.7 | async-start | bytes 1048576 | tf_op jit(solution)/shard_map/all_to_all | solution.py:203
  231.5 18.1 %all-to-all-start.3 = ((bf16[4,256,256]{1,2,0:T(8,128)(2,1)}), bf16[4,256,256]{1,2,0:T(8,128)(2,1)}, u32[]{:S(2)}, u32[]{:S(2)}) async-start(bf16[4,256,256]{1,2,0:T(8,128)(2,1)} %copy.208), calls=%async_computation.3 | async-start | bytes 1048576 | tf_op jit(solution)/shard_map/all_to_all | solution.py:203
  329.0 20.1 %all-to-all-start.12 = ((bf16[256,4,256]{0,2,1:T(8,128)(2,1)}), bf16[256,4,256]{0,2,1:T(8,128)(2,1)}, u32[]{:S(2)}, u32[]{:S(2)}) async-start(bf16[256,4,256]{0,2,1:T(8,128)(2,1)} %bitcast.52), calls=%async_computation.12 | async-start | bytes 1048576 | tf_op jit(solution)/shard_map/all_to_all | solution.py:245
  334.0 261.3 %reduce-scatter.7.cloned.1.call-start = ((), (), s32[]{:S(2)}) async-start(), calls=%async_computation.25 | async-start | bytes 2359296 | tf_op jit(solution)/shard_map/reduce_scatter | solution.py:268
  349.1 54.4 %all-to-all-start.8 = ((bf16[256,4,256]{0,2,1:T(8,128)(2,1)}), bf16[256,4,256]{0,2,1:T(8,128)(2,1)}, u32[]{:S(2)}, u32[]{:S(2)}) async-start(bf16[256,4,256]{0,2,1:T(8,128)(2,1)} %bitcast.41), calls=%async_computation.8 | async-start | bytes 1048576 | tf_op jit(solution)/shard_map/all_to_all | solution.py:245
  403.5 18.7 %all-to-all-start.14 = ((bf16[4,256,256]{1,2,0:T(8,128)(2,1)}), bf16[4,256,256]{1,2,0:T(8,128)(2,1)}, u32[]{:S(2)}, u32[]{:S(2)}) async-start(bf16[4,256,256]{1,2,0:T(8,128)(2,1)} %copy.239), calls=%async_computation.14 | async-start | bytes 1048576 | tf_op jit(solution)/shard_map/all_to_all | solution.py:251
  408.6 186.8 %reduce-scatter.11.cloned.1.call-start = ((), (), s32[]{:S(2)}) async-start(), calls=%async_computation.27 | async-start | bytes 6045696 | tf_op jit(solution)/shard_map/reduce_scatter | solution.py:268
  422.3 47.4 %all-to-all-start.13 = ((bf16[4,256,256]{1,2,0:T(8,128)(2,1)}), bf16[4,256,256]{1,2,0:T(8,128)(2,1)}, u32[]{:S(2)}, u32[]{:S(2)}) async-start(bf16[4,256,256]{1,2,0:T(8,128)(2,1)} %copy.238), calls=%async_computation.13 | async-start | bytes 1048576 | tf_op jit(solution)/shard_map/all_to_all | solution.py:250
  469.6 18.3 %all-to-all-start.10 = ((bf16[4,256,256]{1,2,0:T(8,128)(2,1)}), bf16[4,256,256]{1,2,0:T(8,128)(2,1)S(1)}, u32[]{:S(2)}, u32[]{:S(2)}) async-start(bf16[4,256,256]{1,2,0:T(8,128)(2,1)} %copy.229), calls=%async_computation.10 | async-start | bytes 1048576 | tf_op jit(solution)/shard_map/all_to_all | solution.py:251
  505.1 18.3 %all-to-all-start.11 = ((bf16[4,256,256]{1,2,0:T(8,128)(2,1)}), bf16[4,256,256]{1,2,0:T(8,128)(2,1)}, u32[]{:S(2)}, u32[]{:S(2)}) async-start(bf16[4,256,256]{1,2,0:T(8,128)(2,1)} %copy.230), calls=%async_computation.11 | async-start | bytes 1048576 | tf_op jit(solution)/shard_map/all_to_all | solution.py:252
  523.4 18.2 %all-to-all-start.15 = ((bf16[4,256,256]{1,2,0:T(8,128)(2,1)}), bf16[4,256,256]{1,2,0:T(8,128)(2,1)}, u32[]{:S(2)}, u32[]{:S(2)}) async-start(bf16[4,256,256]{1,2,0:T(8,128)(2,1)} %copy.240), calls=%async_computation.15 | async-start | bytes 1048576 | tf_op jit(solution)/shard_map/all_to_all | solution.py:252
  527.6 83.4 %reduce-scatter.5.cloned.1.call-start = ((), (), s32[]{:S(2)}) async-start(), calls=%async_computation.24 | async-start | bytes 7077888 | tf_op jit(solution)/shard_map/reduce_scatter | solution.py:268
  551.1 146.3 %reduce-scatter.9.cloned.1.call-start = ((), (), s32[]{:S(2)}) async-start(), calls=%async_computation.26 | async-start | bytes 12091392 | tf_op jit(solution)/shard_map/reduce_scatter | solution.py:268
  582.8 237.3 %all-reduce.15.cloned.1.call-start = ((), (), s32[]{:S(2)}) async-start(), calls=%async_computation.28 | async-start | bytes 6127616 | tf_op jit(solution)/shard_map/psum | solution.py:271
  (121 other events, 1658.3 us)
Sparse Core Ops, SparseCore 0:
  9.9 48.2 all-gather.6
  60.0 27.8 all-gather.8
  89.8 64.3 all-gather.10
  160.5 42.1 all-gather.12
  343.1 41.7 reduce-scatter.6
  414.3 57.7 reduce-scatter.10
  551.2 59.8 reduce-scatter.4
  614.5 82.7 reduce-scatter.8
  700.2 119.8 all-reduce.14
where the time goes:
time: 843 us; the launch traced here: 834 us
  waiting for transfers between devices  296 us (35%)
  matrix products  225 us (27%)
  local copies, waits for them, and re-layouts  104 us (12%)
  other arithmetic  77.2 us (9%)
  starting transfers between devices  70.9 us (8%)
  blocking collectives  44.9 us (5%)
  between operations  16.1 us (2%)
    reduce_scatter x4, waiting for transfers between devices, shards(): lax.psum_scatter(as_sent(full_terms), 'fsdp', scatter_dimension=0, tiled=...  102 us
    psum x1, waiting for transfers between devices, shards(): lax.psum(as_sent(shard_terms), 'seq')  80.1 us
    all_gather x1, waiting for transfers between devices, shards(): lax.all_gather(qkv_weight, 'fsdp', axis=0, tiled=True)  31.7 us
    dot_general x2, matrix products, shards(): jnp.dot(normed_two_low.T, grad_joined, preferred_element_type=jnp.float32)  31 us
    dot_general x2, matrix products, shards(): jnp.dot(grad_low, down_full.T, preferred_element_type=jnp.float32)  24.2 us
    all_to_all x2, waiting for transfers between devices, shards(): lax.all_to_all(queries, 'seq', split_axis=1, concat_axis=0, tiled=True)  22.1 us
    dot_general x2, matrix products, shards(): jnp.dot(grad_joined, in_full.T, preferred_element_type=jnp.float32)  20.8 us
    dot_general x2, matrix products, shards(): jnp.dot(normed_low.T, grad_qkv, preferred_element_type=jnp.float32)  17.1 us
  transfers between devices with their start and end apart: 25, of which 15 were waited for; matrix products, arithmetic and copies ran while one was open for 37% of the time, Pallas kernels for 0%

commit v1 on v0

--- a/solution.py
+++ b/solution.py
@@ -3,6 +3,8 @@
 import jax
 import jax.numpy as jnp
 from jax import lax
+from jax.experimental import pallas as pl
+from jax.experimental.pallas import tpu as pltpu
 from jax.sharding import PartitionSpec as P
 
 HEADS = 16
@@ -282,9 +284,579 @@
     )
 
 
+MESH = pl.DeviceIdType.MESH
+ANY = pl.BlockSpec(memory_space=pl.ANY)
+VMEM_BYTES = 60 * 2**20
+BF = jnp.bfloat16
+F32 = jnp.float32
+
+
+def nn(a, b):
+    return lax.dot_general(a, b, (((1,), (0,)), ((), ())), preferred_element_type=F32)
+
+
+def nt(a, b):
+    return lax.dot_general(a, b, (((1,), (1,)), ((), ())), preferred_element_type=F32)
+
+
+def spot():
+    z, f = lax.axis_index("seq"), lax.axis_index("fsdp")
+    core = lax.rem(f, 2)
+    x = lax.rem(f // 2, 2)
+    y = f // 4
+    return z, f, y, x, core
+
+
+def remote(src, dst, send, recv, where):
+    return pltpu.make_async_remote_copy(
+        src_ref=src, dst_ref=dst, send_sem=send, recv_sem=recv, device_id=where, device_id_type=MESH
+    )
+
+
+class Rows:
+    def __init__(self, z, f, core):
+        base = f - core
+        self.work, self.home = [], []
+        for i in range(2):
+            zw, cw = 2 * i + core, z // 2
+            self.work.append((zw, base + cw, (zw == z) & (cw == core)))
+            zh, ch = 2 * core + i, lax.rem(z, 2)
+            self.home.append((zh, base + ch, (zh == z) & (ch == core)))
+        self.z = z
+
+    def greet(self, barrier):
+        count = 0
+        for zt, ft, same in self.work + self.home:
+
+            @pl.when(jnp.logical_not(same))
+            def _():
+                pl.semaphore_signal(barrier, inc=1, device_id=(zt, ft), device_id_type=MESH)
+
+            count = count + jnp.where(same, 0, 1)
+        return count
+
+    def start(self, src, dst, send, recv, local, out):
+        places = self.work if out else self.home
+        slot = lax.rem(self.z, 2) if out else self.z // 2
+        for i, (zt, ft, same) in enumerate(places):
+
+            @pl.when(same)
+            def _(i=i):
+                pltpu.make_async_copy(src.at[i], dst.at[slot], local).start()
+
+            @pl.when(jnp.logical_not(same))
+            def _(i=i, zt=zt, ft=ft):
+                remote(src.at[i], dst.at[slot], send.at[i], recv.at[slot], (zt, ft)).start()
+
+    def wait(self, src, dst, send, recv, local, out):
+        goes, comes = (self.work, self.home) if out else (self.home, self.work)
+        for i, (zt, ft, same) in enumerate(goes):
+
+            @pl.when(same)
+            def _(i=i):
+                pltpu.make_async_copy(src.at[i], dst.at[i], local).wait()
+
+            @pl.when(jnp.logical_not(same))
+            def _(i=i, zt=zt, ft=ft):
+                remote(src.at[i], dst.at[i], send.at[i], recv.at[i], (zt, ft)).wait_send()
+
+        for i, (zt, ft, same) in enumerate(comes):
+
+            @pl.when(jnp.logical_not(same))
+            def _(i=i, zt=zt, ft=ft):
+                remote(src.at[i], dst.at[i], send.at[i], recv.at[i], (zt, ft)).wait_recv()
+
+
+def halves(width):
+    cut = (width // 128 // 2) * 128
+    return pl.ds(0, cut), pl.ds(cut, width - cut)
+
+
+def gather_kernel(*refs):
+    shards, (tok, cot, starts) = refs[:5], refs[5:8]
+    wholes, (tok_o, cot_o, starts_o) = refs[8:13], refs[13:16]
+    ss, rs, ls, es, er, el, ds_, dr = refs[16:]
+    z, f, y, x, core = spot()
+    fx, fy, fc = f + 2 - 4 * x, f + 4 - 8 * y, f + 1 - 2 * core
+    fd = fx + 4 - 8 * y
+    rows = Rows(z, f, core)
+    barrier = pltpu.get_barrier_semaphore()
+    for t in (fx, fy, fc):
+        pl.semaphore_signal(barrier, inc=1, device_id=(z, t), device_id_type=MESH)
+    pl.semaphore_wait(barrier, rows.greet(barrier) + 3)
+
+    def copies(w):
+        whole, shard = wholes[w], shards[w]
+        first, second = halves(shard.shape[1])
+        same = lambda i, cols=None: whole.at[i] if cols is None else whole.at[i, :, cols]
+        plan = [
+            (shard, whole.at[f], fx),
+            (shard, whole.at[f], fy),
+            (shard, whole.at[f], fc),
+            (same(fx, first), same(fx, first), fy),
+            (same(fy, second), same(fy, second), fx),
+            (same(fx), same(fx), fc),
+            (same(fy), same(fy), fc),
+            (same(fd, first), same(fd, first), fc),
+            (same(fd, second), same(fd, second), fc),
+        ]
+        return [
+            remote(s, d, ss.at[w, k], rs.at[w, k], (z, t)) for k, (s, d, t) in enumerate(plan)
+        ]
+
+    every = [copies(w) for w in range(5)]
+    info = remote(starts, starts_o.at[core], ds_.at[0], dr.at[0], (z, fc))
+    info.start()
+    own_info = pltpu.make_async_copy(starts, starts_o.at[core], el.at[2])
+    own_info.start()
+    rows.start(tok, tok_o, es.at[0], er.at[0], el.at[0], True)
+    for w in range(5):
+        for k in range(3):
+            every[w][k].start()
+        pltpu.make_async_copy(shards[w], wholes[w].at[f], ls.at[w]).start()
+    rows.start(cot, cot_o, es.at[1], er.at[1], el.at[1], True)
+    for w in range(5):
+        every[w][0].wait_recv()
+        every[w][3].start()
+        every[w][5].start()
+        every[w][1].wait_recv()
+        every[w][4].start()
+        every[w][6].start()
+    for w in range(5):
+        for k in (3, 4):
+            every[w][k].wait_recv()
+            every[w][k + 4].start()
+    for w in range(5):
+        for k in (2, 5, 6, 7, 8):
+            every[w][k].wait_recv()
+        for k in range(9):
+            every[w][k].wait_send()
+        pltpu.make_async_copy(shards[w], wholes[w].at[f], ls.at[w]).wait()
+    rows.wait(tok, tok_o, es.at[0], er.at[0], el.at[0], True)
+    rows.wait(cot, cot_o, es.at[1], er.at[1], el.at[1], True)
+    info.wait()
+    own_info.wait()
+
+
+def gather_all(shards, tok, cot, starts):
+    dma = pltpu.SemaphoreType.DMA
+    out_shape = [jax.ShapeDtypeStruct((8,) + s.shape, s.dtype) for s in shards] + [
+        jax.ShapeDtypeStruct(tok.shape, tok.dtype),
+        jax.ShapeDtypeStruct(cot.shape, cot.dtype),
+        jax.ShapeDtypeStruct((2,) + starts.shape, starts.dtype),
+    ]
+    return pl.pallas_call(
+        gather_kernel,
+        out_shape=out_shape,
+        in_specs=[ANY] * 8,
+        out_specs=[ANY] * 8,
+        scratch_shapes=[
+            dma((5, 9)), dma((5, 9)), dma((5,)), dma((2, 2)), dma((2, 2)), dma((3,)), dma((1,)), dma((1,)),
+        ],
+        compiler_params=pltpu.CompilerParams(collective_id=1, has_side_effects=True),
+        name="gather_weights_and_rows",
+    )(*shards, tok, cot, starts)
+
+
+CHUNK = 768
+CHUNKS = 16
+
+
+def reduce_kernel(grads, out_rows, in_rows, total, out_home, in_home,
+                  acc, r0, ax, ay, rx, ry, bx, by, r2x, r2y, part, zr, ztmp, zr2, fin,
+                  l0, s0, q0, s1, q1, s2, q2, s3, q3, s4, q4, s5, q5, s6, q6, wsem, es, er, el):
+    z, f, y, x, core = spot()
+    fx, fy, fc = f + 2 - 4 * x, f + 4 - 8 * y, f + 1 - 2 * core
+    rows = Rows(z, f, core)
+    outer = (z == 0) | (z == 3)
+    near = jnp.where(z < 2, 1 - z, 5 - z)
+    across = 3 - z
+    half = CHUNK // 2
+    own = jnp.where(z < 2, 0, 1)
+    barrier = pltpu.get_barrier_semaphore()
+    for t in (fx, fy, fc):
+        pl.semaphore_signal(barrier, inc=1, device_id=(z, t), device_id_type=MESH)
+    pl.semaphore_signal(barrier, inc=1, device_id=(near, f), device_id_type=MESH)
+
+    @pl.when(jnp.logical_not(outer))
+    def _():
+        pl.semaphore_signal(barrier, inc=1, device_id=(across, f), device_id_type=MESH)
+
+    pl.semaphore_wait(barrier, rows.greet(barrier) + 4 + jnp.where(outer, 0, 1))
+    rows.start(out_rows, out_home, es.at[0], er.at[0], el.at[0], False)
+    rows.start(in_rows, in_home, es.at[1], er.at[1], el.at[1], False)
+
+    def cols(t):
+        return pl.ds(pl.multiple_of(t * CHUNK, 128), CHUNK)
+
+    def c0(t):
+        return [
+            pltpu.make_async_copy(grads.at[:, core, :, cols(t)], acc.at[t], l0.at[t]),
+            remote(grads.at[:, 1 - core, :, cols(t)], r0.at[t], s0.at[t], q0.at[t], (z, fc)),
+        ]
+
+    def c1(t):
+        return [
+            remote(ax.at[t], rx.at[t], s1.at[t, 0], q1.at[t, 0], (z, fx)),
+            remote(ay.at[t], ry.at[t], s1.at[t, 1], q1.at[t, 1], (z, fy)),
+        ]
+
+    def c2(t):
+        return [
+            remote(bx.at[t], r2x.at[t], s2.at[t, 0], q2.at[t, 0], (z, fy)),
+            remote(by.at[t], r2y.at[t], s2.at[t, 1], q2.at[t, 1], (z, fx)),
+        ]
+
+    def c3(t):
+        return remote(part.at[t], zr.at[t], s3.at[t], q3.at[t], (near, f))
+
+    def c4(t):
+        return remote(ztmp.at[t], zr2.at[t], s4.at[t], q4.at[t], (across, f))
+
+    def c5(t, h):
+        return [
+            remote(fin.at[t, h], fin.at[t, h], s5.at[t, 0], q5.at[t, 0], (across, f)),
+            remote(fin.at[t, h], fin.at[t, h], s5.at[t, 1], q5.at[t, 1], (near, f)),
+        ]
+
+    def c6(t, h):
+        return remote(fin.at[t, h], fin.at[t, h], s6.at[t], q6.at[t], (near, f))
+
+    def up(v):
+        return v.astype(F32)
+
+    def stage(t, k, body):
+        s = t - k
+
+        @pl.when((s >= 0) & (s < CHUNKS))
+        def _():
+            body(s)
+
+    def begin(t):
+        for c in c0(t):
+            c.start()
+
+    def pair(t):
+        for c in c0(t):
+            c.wait()
+        for i in range(2):
+            o = 2 * i + (1 - x)
+            ax[t, i] = (up(acc[t, o, :, :half]) + up(r0[t, o, :, :half])).astype(BF)
+            o = 2 * (1 - y) + i
+            ay[t, i] = (up(acc[t, o, :, half:]) + up(r0[t, o, :, half:])).astype(BF)
+        for c in c1(t):
+            c.start()
+
+    def cross(t):
+        for c in c1(t):
+            c.wait()
+        o = 2 * (1 - y) + x
+        bx[t] = (up(acc[t, o, :, :half]) + up(r0[t, o, :, :half]) + up(rx[t, 1 - y])).astype(BF)
+        o = 2 * y + (1 - x)
+        by[t] = (up(acc[t, o, :, half:]) + up(r0[t, o, :, half:]) + up(ry[t, 1 - x])).astype(BF)
+        for c in c2(t):
+            c.start()
+
+    def plane(t):
+        for c in c2(t):
+            c.wait()
+        o = 2 * y + x
+        part[t, 0] = (up(acc[t, o, :, :half]) + up(r0[t, o, :, :half]) + up(rx[t, y]) + up(r2x[t])).astype(BF)
+        part[t, 1] = (up(acc[t, o, :, half:]) + up(r0[t, o, :, half:]) + up(ry[t, x]) + up(r2y[t])).astype(BF)
+
+        @pl.when(outer)
+        def _():
+            c3(t).start()
+
+    def meet(t):
+        @pl.when(jnp.logical_not(outer))
+        def _():
+            c3(t).wait_recv()
+            ztmp[t] = (up(part[t, 1 - own]) + up(zr[t, 1 - own])).astype(BF)
+            c4(t).start()
+
+    def sums(t):
+        @pl.when(jnp.logical_not(outer))
+        def _():
+            c4(t).wait()
+            fin[t, own] = (up(part[t, own]) + up(zr[t, own]) + up(zr2[t])).astype(BF)
+            for c in c5(t, own):
+                c.start()
+
+    def spread(t):
+        @pl.when(jnp.logical_not(outer))
+        def _():
+            c5(t, own)[0].wait_recv()
+            c6(t, 1 - own).start()
+
+    def write(t):
+        return [
+            pltpu.make_async_copy(fin.at[t, h], total.at[:, pl.ds(pl.multiple_of(t * CHUNK + h * half, 128), half)], wsem.at[t, h])
+            for h in range(2)
+        ]
+
+    def finish(t):
+        @pl.when(jnp.logical_not(outer))
+        def _():
+            for c in c5(t, own):
+                c.wait_send()
+            c6(t, 1 - own).wait_send()
+
+        @pl.when(outer)
+        def _():
+            c3(t).wait_send()
+            c5(t, own)[1].wait_recv()
+            c6(t, 1 - own).wait_recv()
+
+        for c in write(t):
+            c.start()
+
+    def end(t):
+        for c in write(t):
+            c.wait()
+
+    def body(t, _):
+        stage(t, 0, begin)
+        stage(t, 1, pair)
+        stage(t, 2, cross)
+        stage(t, 3, plane)
+        stage(t, 4, meet)
+        stage(t, 5, sums)
+        stage(t, 6, spread)
+        stage(t, 7, finish)
+        stage(t, 8, end)
+        return 0
+
+    lax.fori_loop(0, CHUNKS + 8, body, 0)
+    rows.wait(out_rows, out_home, es.at[0], er.at[0], el.at[0], False)
+    rows.wait(in_rows, in_home, es.at[1], er.at[1], el.at[1], False)
+
+
+def reduce_all(grads, out_rows, in_rows):
+    dma = pltpu.SemaphoreType.DMA
+    half = CHUNK // 2
+    n = CHUNKS
+    r = 128
+
+    def buf(*s):
+        return pltpu.VMEM(s, BF)
+
+    return pl.pallas_call(
+        reduce_kernel,
+        out_shape=[
+            jax.ShapeDtypeStruct((r, n * CHUNK), BF),
+            jax.ShapeDtypeStruct(out_rows.shape, BF),
+            jax.ShapeDtypeStruct(in_rows.shape, BF),
+        ],
+        in_specs=[ANY] * 3,
+        out_specs=[ANY] * 3,
+        scratch_shapes=[
+            buf(n, 4, r, CHUNK), buf(n, 4, r, CHUNK),
+            buf(n, 2, r, half), buf(n, 2, r, half), buf(n, 2, r, half), buf(n, 2, r, half),
+            buf(n, r, half), buf(n, r, half), buf(n, r, half), buf(n, r, half),
+            buf(n, 2, r, half), buf(n, 2, r, half), buf(n, r, half), buf(n, r, half), buf(n, 2, r, half),
+            dma((n,)), dma((n,)), dma((n,)), dma((n, 2)), dma((n, 2)), dma((n, 2)), dma((n, 2)),
+            dma((n,)), dma((n,)), dma((n,)), dma((n,)), dma((n, 2)), dma((n, 2)), dma((n,)), dma((n,)),
+            dma((n, 2)), dma((2, 2)), dma((2, 2)), dma((2,)),
+        ],
+        compiler_params=pltpu.CompilerParams(
+            collective_id=2, has_side_effects=True, vmem_limit_bytes=VMEM_BYTES
+        ),
+        name="reduce_gradients",
+    )(grads, out_rows, in_rows)
+
+
+def attention_kernel(q_ref, k_ref, v_ref, bias_ref, o_ref, lse_ref):
+    q = q_ref[...] * jnp.asarray(0.125, BF)
+    k = k_ref[...]
+    lane = lax.broadcasted_iota(jnp.int32, (1, 128), 1)
+    vt = v_ref[...].T
+    outs = []
+    for h in range(2):
+        mine = (lane < 64) if h == 0 else (lane >= 64)
+        scores = nt(k, jnp.where(mine, q, jnp.zeros_like(q))) + bias_ref[...]
+        top = jnp.max(scores, axis=0, keepdims=True)
+        p = jnp.exp(scores - top)
+        total = jnp.sum(p, axis=0, keepdims=True)
+        outs.append(nn(vt, p.astype(BF)) / total)
+        lse_ref[0, h : h + 1, :] = top + jnp.log(total)
+    o_ref[...] = jnp.concatenate([outs[0][:64], outs[1][64:]], axis=0).T.astype(BF)
+
+
+def attention_back_kernel(q_ref, k_ref, v_ref, bias_ref, o_ref, do_ref, lse_ref, dq_ref, dk_ref, dv_ref):
+    q = q_ref[...] * jnp.asarray(0.125, BF)
+    k, v, do = k_ref[...], v_ref[...], do_ref[...]
+    lane = lax.broadcasted_iota(jnp.int32, (1, 128), 1)
+    kt = k.T
+    products = (o_ref[...].astype(F32) * do.astype(F32)).T
+    none = jnp.zeros_like(q)
+    dqs, dks, dvs = [], [], []
+    for h in range(2):
+        mine = (lane < 64) if h == 0 else (lane >= 64)
+        centre = jnp.sum(products[64 * h : 64 * h + 64], axis=0, keepdims=True)
+        p = jnp.exp(nt(k, jnp.where(mine, q, none)) + bias_ref[...] - lse_ref[0, h : h + 1, :])
+        dvs.append(nn(p.astype(BF), do))
+        ds = (p * (nt(v, jnp.where(mine, do, none)) - centre)).astype(BF)
+        dks.append(nn(ds, q))
+        dqs.append(nn(kt, ds))
+    dq = jnp.concatenate([dqs[0][:64], dqs[1][64:]], axis=0).T
+    dq_ref[...] = (dq * 0.125).astype(BF)
+    dk_ref[...] = jnp.where(lane < 64, dks[0], dks[1]).astype(BF)
+    dv_ref[...] = jnp.where(lane < 64, dvs[0], dvs[1]).astype(BF)
+
+
+def attention(q, k, v, bias):
+    rows, keys = q.shape[0], k.shape[0]
+    narrow = pl.BlockSpec((rows, 128), lambda i: (0, i))
+    long = pl.BlockSpec((keys, 128), lambda i: (0, i))
+    return pl.pallas_call(
+        attention_kernel,
+        grid=(q.shape[1] // 128,),
+        in_specs=[narrow, long, long, pl.BlockSpec((keys, rows), lambda i: (0, 0))],
+        out_specs=[narrow, pl.BlockSpec((1, 2, rows), lambda i: (i, 0, 0))],
+        out_shape=[
+            jax.ShapeDtypeStruct(q.shape, BF),
+            jax.ShapeDtypeStruct((q.shape[1] // 128, 2, rows), F32),
+        ],
+        compiler_params=pltpu.CompilerParams(vmem_limit_bytes=VMEM_BYTES),
+        name="attention",
+    )(q, k, v, bias)
+
+
+def attention_back(q, k, v, bias, o, do, lse):
+    rows, keys = q.shape[0], k.shape[0]
+    narrow = pl.BlockSpec((rows, 128), lambda i: (0, i))
+    long = pl.BlockSpec((keys, 128), lambda i: (0, i))
+    return pl.pallas_call(
+        attention_back_kernel,
+        grid=(q.shape[1] // 128,),
+        in_specs=[narrow, long, long, pl.BlockSpec((keys, rows), lambda i: (0, 0)), narrow, narrow,
+                  pl.BlockSpec((1, 2, rows), lambda i: (i, 0, 0))],
+        out_specs=[narrow, long, long],
+        out_shape=[jax.ShapeDtypeStruct(q.shape, BF)] + [jax.ShapeDtypeStruct(k.shape, BF)] * 2,
+        compiler_params=pltpu.CompilerParams(vmem_limit_bytes=VMEM_BYTES),
+        name="attention_back",
+    )(q, k, v, bias, o, do, lse)
+
+
+def turn_rows(values, cosine, sine, back):
+    shaped = values.reshape(values.shape[0], -1, HEAD_DIM)
+    if back:
+        g = shaped * sine
+        half = HEAD_DIM // 2
+        turned = jnp.concatenate([g[..., half:], -g[..., :half]], axis=-1)
+        return (shaped * cosine + turned).reshape(values.shape)
+    return rotate(shaped, cosine, sine).reshape(values.shape)
+
+
+def swap(value):
+    return lax.ppermute(value, "fsdp", [(i, i ^ 1) for i in range(lax.axis_size("fsdp"))])
+
+
+def chip_streams(tokens, cotangent, doc_starts, qkv_weight, out_weight, in_weight, down_weight, attn_gain, ffn_gain):
+    z, core = lax.axis_index("seq"), lax.axis_index("fsdp") % 2
+    wide = tokens.shape[3]
+    gains = jnp.concatenate([attn_gain, ffn_gain])[None] + jnp.zeros((16, 1), BF)
+    starts = jnp.zeros((8, 128), jnp.int32).at[:2, :8].set(doc_starts[:, 0])
+    shards_in = (gains, qkv_weight, out_weight, in_weight, down_weight)
+    gains_f, qkv_f, out_f, in_f, down_f, tok_r, cot_r, starts_r = gather_all(
+        shards_in, tokens[:, 0].astype(BF), cotangent[:, 0].astype(BF), starts
+    )
+    gain_one = gains_f[:, 0, :128].reshape(wide).astype(F32)
+    gain_two = gains_f[:, 0, 128:].reshape(wide).astype(F32)
+    qkv_full, out_full, in_full, down_full = (
+        w.reshape(-1, w.shape[-1]) for w in (qkv_f, out_f, in_f, down_f)
+    )
+    rows_in = tok_r.reshape(-1, wide).astype(F32)
+    grad_low = cot_r.reshape(-1, wide)
+    grad_out = grad_low.astype(F32)
+    count = rows_in.shape[0]
+    mine = starts_r[z % 2, z // 2, :8]
+    here = core * count + jnp.arange(count, dtype=jnp.int32)
+    there = (1 - core) * count + jnp.arange(count, dtype=jnp.int32)
+    cosine, sine = (t[:, None, :] for t in rope_tables(mine, here, HEAD_DIM))
+    seg_here, seg_there = segment_ids(mine, here), segment_ids(mine, there)
+    bias = jnp.where(
+        jnp.concatenate([seg_here, seg_there])[:, None] == seg_here[None, :], 0.0, MASKED_SCORE
+    ).astype(F32)
+
+    normed, norm_back = jax.vjp(layer_norm, rows_in, gain_one)
+    normed_low = normed.astype(BF)
+    qkv = nn(normed_low, qkv_full)
+    q = turn_rows(qkv[:, :wide], cosine, sine, False).astype(BF)
+    k = turn_rows(qkv[:, wide : 2 * wide], cosine, sine, False).astype(BF)
+    v = qkv[:, 2 * wide :].astype(BF)
+    k_all = jnp.concatenate([k, swap(k)])
+    v_all = jnp.concatenate([v, swap(v)])
+    mixture, lse = attention(q, k_all, v_all, bias)
+    middle = rows_in + nn(mixture, out_full)
+    normed_two, norm_back_two = jax.vjp(layer_norm, middle, gain_two)
+    normed_two_low = normed_two.astype(BF)
+    joined = nn(normed_two_low, in_full)
+    active, gelu_back = jax.vjp(gated_gelu, joined)
+    active_low = active.astype(BF)
+    output = middle + nn(active_low, down_full)
+
+    down_term = nn(active_low.T, grad_low)
+    grad_active = nt(grad_low, down_full)
+    grad_joined = gelu_back(grad_active)[0].astype(BF)
+    in_term = nn(normed_two_low.T, grad_joined)
+    grad_normed_two = nt(grad_joined, in_full)
+    grad_middle_norm, gain_two_term = norm_back_two(grad_normed_two)
+    grad_middle = grad_out + grad_middle_norm
+    grad_mid_low = grad_middle.astype(BF)
+    out_term = nn(mixture.T, grad_mid_low)
+    grad_mixture = nt(grad_mid_low, out_full).astype(BF)
+    dq, dk, dv = attention_back(q, k_all, v_all, bias, mixture, grad_mixture, lse)
+    dk = (dk[:count].astype(F32) + swap(dk[count:]).astype(F32)).astype(BF).astype(F32)
+    dv = (dv[:count].astype(F32) + swap(dv[count:]).astype(F32)).astype(BF)
+    grad_qkv = jnp.concatenate(
+        [
+            turn_rows(dq.astype(F32), cosine, sine, True).astype(BF),
+            turn_rows(dk, cosine, sine, True).astype(BF),
+            dv,
+        ],
+        axis=1,
+    )
+    qkv_term = nn(normed_low.T, grad_qkv)
+    grad_normed = nt(grad_qkv, qkv_full)
+    grad_rows, gain_one_term = norm_back(grad_normed)
+    tokens_grad = grad_middle + grad_rows
+
+    gain_terms = jnp.concatenate(
+        [gain_one_term.reshape(8, 1, 128), gain_two_term.reshape(8, 1, 128)], axis=2
+    )
+    parts = [
+        qkv_term.reshape(8, 128, -1).astype(BF),
+        out_term.reshape(8, 128, -1).astype(BF),
+        in_term.reshape(8, 128, -1).astype(BF),
+        down_term.reshape(8, 128, -1).astype(BF),
+        (gain_terms + jnp.zeros((1, 128, 1))).astype(BF),
+    ]
+    used = sum(p.shape[2] for p in parts)
+    parts.append(jnp.zeros((8, 128, CHUNK * CHUNKS - used), BF))
+    grads = jnp.concatenate(parts, axis=2).reshape(4, 2, 128, CHUNK * CHUNKS)
+    total, out_home, in_home = reduce_all(
+        grads, output.astype(BF).reshape(2, -1, wide), tokens_grad.astype(BF).reshape(2, -1, wide)
+    )
+    total = total.astype(F32)
+    a, b, c, d = 3 * wide, 4 * wide, 4 * wide + in_weight.shape[1], used - 256
+    return (
+        out_home[:, None].astype(F32),
+        in_home[:, None].astype(F32),
+        total[:, :a],
+        total[:, a:b],
+        total[:, b:c],
+        total[:, c:d].reshape(down_weight.shape),
+        total[0, d : d + 128],
+        total[0, d + 128 : d + 256],
+    )
+
+
 def solution(mesh):
+    whole_chips = dict(mesh.shape) == {"seq": 4, "fsdp": 8}
     return jax.shard_map(
-        shards,
+        chip_streams if whole_chips else shards,
         mesh=mesh,
         in_specs=(
             P(None, "fsdp", "seq", None),

time: 843 us -> 594 us (0.70)
  Pallas kernels: 0 us -> 325 us
  waiting for transfers between devices: 296 us -> 0.01 us
  matrix products: 225 us -> 92.4 us
  starting transfers between devices: 70.9 us -> 1.08 us
  blocking collectives: 44.9 us -> 0 us
  between operations: 16.1 us -> 1.37 us
  other arithmetic: 77.2 us -> 66.4 us
    pallas_call x0 -> x4, Pallas kernels: none -> 325 us  [the longest x1 151 us: reduce_all(): pl.pallas_call(reduce_kernel, out_shape=[jax.ShapeDtypeStruct((r, n * CHU...]
    dot_general x52 -> x12, matrix products: 225 us -> 92.4 us  [the longest x8 57.5 us: nn(): lax.dot_general(a, b, (((1,), (0,)), ((), ())), preferred_element_type=F32)]
    reduce_scatter x4 -> x0, waiting for transfers between devices: 102 us -> none  [shards(): lax.psum_scatter(as_sent(full_terms), 'fsdp', scatter_dimension=0, tiled=...]
    psum x1 -> x0, waiting for transfers between devices: 80.1 us -> none  [shards(): lax.psum(as_sent(shard_terms), 'seq')]
    all_to_all x16 -> x0, waiting for transfers between devices: 79.3 us -> none  [the longest x2 22.1 us: shards(): lax.all_to_all(queries, 'seq', split_axis=1, concat_axis=0, tiled=True)]
    all_to_all x16 -> x0, starting transfers between devices: 70.2 us -> none  [the longest x2 10.6 us: shards(): lax.all_to_all(mixture.astype(jnp.bfloat16), 'seq', split_axis=0, concat_...]
    concatenate x0 -> x3, local copies, waits for them, and re-layouts: none -> 48.1 us  [the longest x1 42.3 us: chip_streams(): grads = jnp.concatenate(parts, axis=2).reshape(4, 2, 128, CHUNK * CHUNKS)]
    all_gather x4 -> x0, waiting for transfers between devices: 31.8 us -> none  [the longest x1 31.7 us: shards(): lax.all_gather(qkv_weight, 'fsdp', axis=0, tiled=True)]
  transfers between devices with their start and end apart: 25 -> 4, of which waited for: 15 -> 0; matrix products, arithmetic and copies ran while one was open for 37% -> 10% of each run, Pallas kernels for 0% -> 0%
where the time goes in v1:
time: 594 us; the launch traced here: 589 us
  Pallas kernels  325 us (55%)
  local copies, waits for them, and re-layouts  103 us (17%)
  matrix products  92.4 us (16%)
  other arithmetic  66.4 us (11%)
    pallas_call x1, Pallas kernels, reduce_all(): pl.pallas_call(reduce_kernel, out_shape=[jax.ShapeDtypeStruct((r, n * CHU...  151 us
    pallas_call x1, Pallas kernels, gather_all(): pl.pallas_call(gather_kernel, out_shape=out_shape, in_specs=[ANY] * 8, ou...  131 us
    dot_general x8, matrix products, nn(): lax.dot_general(a, b, (((1,), (0,)), ((), ())), preferred_element_type=F32)  57.5 us
    concatenate x1, local copies, waits for them, and re-layouts, chip_streams(): grads = jnp.concatenate(parts, axis=2).reshape(4, 2, 128, CHUNK * CHUNKS)  42.3 us
    dot_general x4, matrix products, nt(): lax.dot_general(a, b, (((1,), (1,)), ((), ())), preferred_element_type=F32)  35 us
    pallas_call x1, Pallas kernels, attention_back(): pl.pallas_call(attention_back_kernel, grid=(q.shape[1] // 128,), in_specs...  25.4 us
    pallas_call x1, Pallas kernels, attention(): pl.pallas_call(attention_kernel, grid=(q.shape[1] // 128,), in_specs=[nar...  18.3 us
    convert_element_type x1, other arithmetic, chip_streams(): active_low = active.astype(BF)  13.6 us
  transfers between devices with their start and end apart: 4, of which 0 were waited for; matrix products, arithmetic and copies ran while one was open for 10% of the time, Pallas kernels for 0%

profile of v1, /device:TPU:0, one launch (start us, length us, event | category | flops | bytes accessed | tf_op | source)
XLA Modules:
  0.0 589.2 jit_solution(15401287533174463933)
XLA Ops:
  2.0 3.9 fusion.25
  6.5 131.1 %gather_weights_and_rows.1 = (bf16[8,16,256]{2,1,0:T(8,128)(2,1)}, bf16[8,128,3072]{2,1,0:T(8,128)(2,1)}, bf16[8,128,1024]{2,1,0:T(8,128)(2,1)}, bf16[8,128,5248...) custom-call(bf16[16,256]{1,0:T(8,128)(2,1)} %add.119.refs_0_, ...), custom_call_target="tpu_custom_call" | custom-call | tf_op jit(solution)/shard_map/gather_weights_and_rows/pallas_call | solution.py:448
  141.8 5.8 fusion.48
  160.6 2.9 copy.47
  168.8 6.4 %add_convert_fusion.7 = (bf16[512,1024]{1,0:T(8,128)(2,1)S(1)}, bf16[512,1024]{1,0:T(8,128)(2,1)}) fusion(f32[512,1024]{1,0:T(8,128)} %copy.50, f32[512,1024]{1,0:T(8,128)S(1)} %copy.45, f32[512,3072]{1,0:T(8,128)} %copy-done.4, f32[512,1024]{1,0:T(8,128)} %copy.47), kind=kLoop, calls=%fused_computation.64 | loop fusion | flops 3145728 | bytes 12582912 | tf_op jit(solution)/shard_map/convert_element_type | solution.py:787
  182.0 18.3 %attention.1 = (bf16[512,1024]{1,0:T(8,128)(2,1)}, f32[8,2,512]{2,1,0:T(2,128)}) custom-call(bf16[512,1024]{1,0:T(8,128)(2,1)} %get-tuple-element.90.q_ref, bf16[1024,1024]{1,0:T(8,128)(2,1)} %pad_maximum_fusion.1.k_ref, bf16[1024,1024]{1,0:T(8,128)(2,1)} %pad_maximum_fusion.2.v_ref, f32[1024,512]{1,0:T(8,128)} %compare_select_fusion.bias_ref), custom_call_target="tpu_custom_call" | custom-call | tf_op jit(solution)/shard_map/attention/pallas_call | solution.py:712
  200.4 3.3 fusion.47
  204.0 9.2 %fusion.41 = f32[512,5248]{1,0:T(8,128)S(1)} fusion(bf16[1024,5248]{1,0:T(8,128)(2,1)} %bitcast.151, f32[512,1024]{1,0:T(8,128)S(1)} %get-tuple-element.122, f32[1024]{0:T(1024)S(1)} %bitcast.143, f32[512]{0:T(512)S(1)} %fusion.32, f32[512]{0:T(512)S(1)} %broadcast_multiply_fusion.3), kind=kOutput, calls=%fused_computation.126 | convolution fusion | flops 5505024000 | bytes 23601152 | tf_op jit(solution)/shard_map/dot_general | solution.py:295
  213.2 13.6 %multiply_convert_fusion = (bf16[512,2624]{1,0:T(8,128)(2,1)}, f32[512,2624]{1,0:T(8,128)S(1)}) fusion(f32[512,5248]{1,0:T(8,128)S(1)} %fusion.41), kind=kLoop, calls=%fused_computation.6 | loop fusion | flops 88670208 | bytes 18808832 | tf_op jit(solution)/shard_map/convert_element_type | solution.py:797
  226.8 12.5 %fusion.21 = (f32[512,2624]{1,0:T(8,128)}, f32[512,2624]{1,0:T(8,128)}) fusion(f32[512,2624]{1,0:T(8,128)S(1)} %get-tuple-element.84, f32[512,5248]{1,0:T(8,128)} %copy-done.5, bf16[512,1024]{1,0:T(8,128)(2,1)S(1)} %bitcast.129, bf16[2624,1024]{1,0:T(8,128)(2,1)} %bitcast.155), kind=kOutput, calls=%fused_computation.68 | convolution fusion | flops 2772959232 | bytes 33292288 | tf_op jit(solution)/shard_map/dot_general | solution.py:299
  239.3 13.1 %multiply_reduce_fusion = (bf16[1024]{0:T(1024)(128)(2,1)S(1)}, f32[512]{0:T(512)S(1)}, f32[512,1024]{1,0:T(8,128)}) fusion(f32[512,1024]{1,0:T(8,128)S(1)} %get-tuple-element.122, f32[512]{0:T(512)S(1)} %fusion.32, f32[512]{0:T(512)S(1)} %broadcast_multiply_fusion.3, f32[1024]{0:T(1024)S(1)} %bitcast.144, bf16[1024,5248]{1,0:T(8,128)(2,1)} %bitcast.152, ...), kind=kOutput, calls=%fused_computation.55 | convolution fusion | flops 5511969280 | bytes 25702400 | tf_op jit(solution)/shard_map/dot_general | solution.py:299
  252.4 13.4 %convolution_convert_fusion = bf16[1024,5248]{1,0:T(8,128)(2,1)} fusion(f32[512,2624]{1,0:T(8,128)} %get-tuple-element.88, f32[512,2624]{1,0:T(8,128)} %get-tuple-element.87, f32[512,1024]{1,0:T(8,128)S(1)} %get-tuple-element.122, f32[1024]{0:T(1024)S(1)} %bitcast.145, f32[512]{0:T(512)S(1)} %fusion.32, f32[512]{0:T(512)S(1)} %broadcast_multiply_fusion.3), kind=kOutput, calls=%fused_computation | convolution fusion | flops 5515771904 | bytes 23601152 | tf_op jit(solution)/shard_map/dot_general | solution.py:295
  274.8 25.4 %attention_back.1 = (bf16[512,1024]{1,0:T(8,128)(2,1)}, bf16[1024,1024]{1,0:T(8,128)(2,1)}, bf16[1024,1024]{1,0:T(8,128)(2,1)}) custom-call(bf16[512,1024]{1,0:T(8,128)(2,1)} %get-tuple-element.90.q_ref, bf16[1024,1024]{1,0:T(8,128)(2,1)} %pad_maximum_fusion.1.k_ref, bf16[1024,1024]{1,0:T(8,128)(2,1)} %pad_maximum_fusion.2.v_ref, ...), custom_call_target="tpu_custom_call" | custom-call | tf_op jit(solution)/shard_map/attention_back/pallas_call | solution.py:730
  307.8 6.5 %convolution_convert_fusion.1 = bf16[2624,1024]{1,0:T(8,128)(2,1)} fusion(bf16[512,2624]{1,0:T(8,128)(2,1)} %get-tuple-element.83, bf16[512,1024]{1,0:T(8,128)(2,1)S(1)} %bitcast.130), kind=kOutput, calls=%fused_computation.3 | convolution fusion | flops 2754150400 | bytes 9109504 | tf_op jit(solution)/shard_map/dot_general | solution.py:295
  314.4 11.6 %convert_element_type.205 = bf16[8,128,2624]{2,1,0:T(8,128)(2,1)} reshape(bf16[2624,1024]{1,0:T(8,128)(2,1)} %convolution_convert_fusion.1) | data formatting | bytes 10747904 | tf_op jit(solution)/shard_map/convert_element_type | solution.py:833
  326.0 8.2 %add_convert_fusion.2 = bf16[512,1024]{1,0:T(8,128)(2,1)} fusion(f32[512,1024]{1,0:T(8,128)} %copy-done.6, bf16[512,2624]{1,0:T(8,128)(2,1)} %get-tuple-element.83, bf16[2624,1024]{1,0:T(8,128)(2,1)} %bitcast.156), kind=kOutput, calls=%fused_computation.54 | convolution fusion | flops 2752512000 | bytes 11206656 | tf_op jit(solution)/shard_map/dot_general | solution.py:295
  334.2 2.9 fusion.24
  337.2 3.1 copy.57
  340.2 4.3 broadcast_multiply_fusion.1
  357.7 4.3 add_convert_fusion.6
  362.1 7.1 %fusion.20 = (f32[512]{0:T(512)S(1)}, f32[512,1024]{1,0:T(8,128)S(1)}) fusion(bf16[2,256,1024]{2,1,0:T(8,128)(2,1)S(1)} %copy-done.1, f32[1024]{0:T(1024)S(1)} %bitcast.137, f32[512]{0:T(512)S(1)} %bitcast.140, bf16[1024,3072]{1,0:T(8,128)(2,1)} %bitcast.154, bf16[512,1024]{1,0:T(8,128)(2,1)S(1)} %add_convert_fusion.3, ...), kind=kOutput, calls=%fused_computation.50 | convolution fusion | flops 3233283584 | bytes 12591104 | tf_op jit(solution)/shard_map/dot_general | solution.py:299
  375.0 8.4 %convolution_convert_fusion.2 = bf16[8,128,3072]{2,1,0:T(8,128)(2,1)} fusion(bf16[8,128,512]{2,1,0:T(8,128)(2,1)} %bitcast.133, bf16[512,1024]{1,0:T(8,128)(2,1)} %copy-done.18, bf16[512,1024]{1,0:T(8,128)(2,1)} %copy-done.22, bf16[512,1024]{1,0:T(8,128)(2,1)} %copy-done.21), kind=kOutput, calls=%fused_computation.4 | convolution fusion | flops 3233808384 | bytes 10485760 | tf_op jit(solution)/shard_map/dot_general | solution.py:295
  383.5 42.3 %concatenate.64 = bf16[8,128,12288]{2,1,0:T(8,128)(2,1)} concatenate(bf16[8,128,3072]{2,1,0:T(8,128)(2,1)} %convolution_convert_fusion.2, bf16[8,128,1024]{2,1,0:T(8,128)(2,1)S(1)} %bitcast.132, bf16[8,128,5248]{2,1,0:T(8,128)(2,1)} %bitcast.118, bf16[8,128,2624]{2,1,0:T(8,128)(2,1)} %convert_element_type.205, bf16[8,128,256]{2,1,0:T(8,128)(2,1)S(1)} %add.139, ...), dimensions={2} | concatenate | bytes 50331648 | tf_op jit(solution)/shard_map/concatenate | solution.py:838
  425.8 150.7 %reduce_gradients.1 = (bf16[128,12288]{1,0:T(8,128)(2,1)}, bf16[2,256,1024]{2,1,0:T(8,128)(2,1)}, bf16[2,256,1024]{2,1,0:T(8,128)(2,1)}) custom-call(bf16[4,2,128,12288]{3,2,1,0:T(8,128)(2,1)} %bitcast.117, bf16[2,256,1024]{2,1,0:T(8,128)(2,1)} %bitcast.135, bf16[2,256,1024]{2,1,0:T(8,128)(2,1)} %bitcast.131), custom_call_target="tpu_custom_call" | custom-call | tf_op jit(solution)/shard_map/reduce_gradients/pallas_call | solution.py:644
  (130 shorter events, 79.5 us)
Async XLA Ops:
  2.0 3.9 copy-start.24
  2.0 3.9 copy-start.25
  137.6 2.7 copy-start.1
  147.7 4.1 copy-start.4
  168.8 6.4 %copy-start.2 = (f32[512,1024]{1,0:T(8,128)}, f32[512,1024]{1,0:T(8,128)S(1)}, u32[]{:S(2)}) copy-start(f32[512,1024]{1,0:T(8,128)S(1)} %copy.45) | copy-start | bytes 6291460
  175.2 3.9 collective-permute-start
  176.9 3.6 collective-permute-start.1
  203.6 48.8 %copy-start.6 = (f32[512,1024]{1,0:T(8,128)}, f32[512,1024]{1,0:T(8,128)S(1)}, u32[]{:S(2)}) copy-start(f32[512,1024]{1,0:T(8,128)S(1)} %get-tuple-element.122) | copy-start | bytes 6291460
  213.2 13.6 %copy-start.5 = (f32[512,5248]{1,0:T(8,128)}, f32[512,5248]{1,0:T(8,128)S(1)}, u32[]{:S(2)}) copy-start(f32[512,5248]{1,0:T(8,128)S(1)} %fusion.41) | copy-start | bytes 32243716
  213.2 13.6 %copy-start.8 = (bf16[2,256,1024]{2,1,0:T(8,128)(2,1)S(1)}, bf16[2,256,1024]{2,1,0:T(8,128)(2,1)}, u32[]{:S(2)}) copy-start(bf16[2,256,1024]{2,1,0:T(8,128)(2,1)} %get-tuple-element.41) | copy-start | bytes 3145732
  252.4 13.5 %copy-start.16 = (f32[512,1024]{1,0:T(8,128)S(1)}, f32[512,1024]{1,0:T(8,128)}, u32[]{:S(2)}) copy-start(f32[512,1024]{1,0:T(8,128)} %get-tuple-element.123) | copy-start | bytes 6291460
  265.8 2.4 copy-start.9
  269.9 2.3 copy-start.17
  302.4 31.8 %collective-permute-start.2 = (bf16[512,1024]{1,0:T(8,128)(2,1)}, bf16[512,1024]{1,0:T(8,128)(2,1)}, u32[]{:S(2)}, u32[]{:S(2)}) collective-permute-start(bf16[512,1024]{1,0:T(8,128)(2,1)} %slice.110), channel_id=1, source_target_pairs={{0,1},{1,0},{2,3},{3,2},{4,5},{5,4},{6,7},{7,6},{8,9},{9,8},{10,11... | collective-permute-start | bytes 3145736 | tf_op jit(solution)/shard_map/ppermute | solution.py:753
  305.0 2.8 copy-start.10
  307.4 47.9 %collective-permute-start.3 = (bf16[512,1024]{1,0:T(8,128)(2,1)}, bf16[512,1024]{1,0:T(8,128)(2,1)}, u32[]{:S(2)}, u32[]{:S(2)}) collective-permute-start(bf16[512,1024]{1,0:T(8,128)(2,1)} %slice.114), channel_id=1, source_target_pairs={{0,1},{1,0},{2,3},{3,2},{4,5},{5,4},{6,7},{7,6},{8,9},{9,8},{10,11... | collective-permute-start | bytes 3145736 | tf_op jit(solution)/shard_map/ppermute | solution.py:753
  326.0 8.2 %copy-start.7 = (bf16[1024,1024]{1,0:T(8,128)(2,1)S(1)}, bf16[1024,1024]{1,0:T(8,128)(2,1)}, u32[]{:S(2)}) copy-start(bf16[1024,1024]{1,0:T(8,128)(2,1)} %get-tuple-element.47) | copy-start | bytes 6291460
  355.2 2.5 copy-start.12
  357.7 4.4 copy-start.18
  362.1 7.2 %copy-start.21 = (bf16[512,1024]{1,0:T(8,128)(2,1)}, bf16[512,1024]{1,0:T(8,128)(2,1)S(1)}, u32[]{:S(2)}) copy-start(bf16[512,1024]{1,0:T(8,128)(2,1)S(1)} %get-tuple-element.95) | copy-start | bytes 3145732
  362.1 7.1 %copy-start.22 = (bf16[512,1024]{1,0:T(8,128)(2,1)}, bf16[512,1024]{1,0:T(8,128)(2,1)S(1)}, u32[]{:S(2)}) copy-start(bf16[512,1024]{1,0:T(8,128)(2,1)S(1)} %get-tuple-element.96) | copy-start | bytes 3145732
  375.0 8.5 %copy-start.15 = (bf16[1024,1024]{1,0:T(8,128)(2,1)S(1)}, bf16[1024,1024]{1,0:T(8,128)(2,1)}, u32[]{:S(2)}) copy-start(bf16[1024,1024]{1,0:T(8,128)(2,1)} %convolution_convert_fusion.3) | copy-start | bytes 6291460
  576.5 2.8 copy-start
  582.4 3.4 copy-start.20
  (6 other events, 9.4 us)
